TPU v7x, 256 devices: a whole 4x4x8 slice. The times are simulated.
256 devices in a mesh: dom: 16 (over y, x), feat: 16 (over z, core).
Axes of the slice: x: 4, y: 4, z: 8, core: 2. Of those that a mesh axis runs over, the one named last changes fastest.
Arguments:
- feature_table: float32 [1024, 131072], P('feat', 'dom'), may hold values from -6 to 6
- seed_ids: int32 [16384], P('dom'), may hold values from 0 to 8191
- neighbours: int32 [15, 16384], P(None, 'dom'), may hold values from 0 to 8191
- owners: int32 [1024, 1], P('dom'), may hold values from 0 to 15; in each aligned block of 64 rows (0 to 63, 64 to 127, ...) at most 8 rows name the same one
- blocks: int32 [1024], P('dom'), may hold values from 0 to 63
- counts: int32 [1024], P('dom'), may hold values from 1 to 128
- w_self: float32 [1024, 1024], P('feat'), may hold values from -0.1875 to 0.1875
- w_neigh: float32 [1024, 1024], P('feat'), may hold values from -0.5 to 0.5
- out_bias: float32 [1024], replicated, may hold values from -3 to 3
- cotangent: bfloat16 [16384, 1024], P(('dom', 'feat')), may hold values from -0.046875 to 0.046875
Outputs:
- hidden: bfloat16 [16384, 1024], P(('dom', 'feat'))
- grad_self: float32 [1024, 1024], P('feat')
- grad_neigh: float32 [1024, 1024], P('feat')
Inputs may be any that keep to these rules, and one draw needn't show every extreme that they name: `owners`: among the 64 frontier entries of one partition no owner appears more than 8 times.
All inputs are finite; a program needn't handle non-finite values.
Results may differ from a plain program's by a relative error of at most 0.003.
Values may be sent and summed in bfloat16 or wider, within the bound.
No kernel may reach another device: no remote copies, remote signals or barrier semaphores. Data moves between devices by JAX's collectives and lax.ppermute only.
A program may use at most 128 MiB of HBM per device.

v0:
```python
import jax
import jax.numpy as jnp
from jax import lax
from jax.sharding import PartitionSpec as P

FAN = 15
BLOCK = 128
SLOTS = 8


def silu_slope(preact):
    sigma = jax.nn.sigmoid(preact)
    return sigma * (1.0 + preact * (1.0 - sigma))


def contract(left, right):
    return lax.dot_general(
        left,
        right,
        (((0,), (0,)), ((), ())),
        precision=lax.Precision.HIGHEST,
        preferred_element_type=jnp.float32,
    )


def product(left, right):
    return lax.dot_general(
        left,
        right,
        (((1,), (0,)), ((), ())),
        precision=lax.Precision.HIGHEST,
        preferred_element_type=jnp.float32,
    )


def body(
    feature_table,
    seed_ids,
    neighbours,
    owners,
    blocks,
    counts,
    w_self,
    w_neigh,
    out_bias,
    cotangent,
):
    cols_dev = feature_table.shape[0]
    node_rows = feature_table.shape[1]
    n_dom = lax.axis_size("dom")
    front = owners.shape[0]
    seeds_dev = seed_ids.shape[0]
    fanout = neighbours.shape[0]
    owner_ids = owners[:, 0]
    one_hot = (owner_ids[:, None] == jnp.arange(n_dom, dtype=jnp.int32)[None, :]).astype(jnp.int32)
    slot_rank = jnp.sum(jnp.cumsum(one_hot, axis=0) * one_hot, axis=1) - 1
    outgoing_ids = jnp.zeros((n_dom, SLOTS), jnp.int32).at[owner_ids, slot_rank].set(blocks)
    requested = lax.all_to_all(outgoing_ids, "dom", split_axis=0, concat_axis=0, tiled=True)
    table_rows = jnp.transpose(feature_table)
    block_rows = table_rows.reshape(node_rows // BLOCK, BLOCK, cols_dev)
    outgoing = block_rows[requested.reshape(-1)].reshape(n_dom, SLOTS, BLOCK, cols_dev)
    arrived = lax.all_to_all(outgoing, "dom", split_axis=0, concat_axis=0, tiled=True)
    arrived_flat = arrived.reshape(n_dom * SLOTS, BLOCK, cols_dev)
    frontier = arrived_flat[owner_ids * SLOTS + slot_rank]
    row_valid = jnp.arange(BLOCK, dtype=jnp.int32)[None, :] < counts[:, None]
    frontier = jnp.where(row_valid[:, :, None], frontier, 0.0).reshape(front * BLOCK, cols_dev)
    picked = frontier[neighbours.reshape(-1)].reshape(fanout, seeds_dev, cols_dev)
    neighbour_mean = jnp.sum(picked, axis=0) * (1.0 / FAN)
    self_rows = table_rows[seed_ids]
    stacked = jnp.concatenate([self_rows, neighbour_mean], axis=1)
    weight_cat = jnp.concatenate([w_self, w_neigh], axis=0)
    preact = (
        lax.psum_scatter(product(stacked, weight_cat), "feat", scatter_dimension=0, tiled=True)
        + out_bias[None, :]
    )
    hidden = jax.nn.silu(preact).astype(jnp.bfloat16)
    slope = (cotangent.astype(jnp.float32) * silu_slope(preact)).astype(jnp.bfloat16)
    grad_local = contract(
        stacked, lax.all_gather(slope, "feat", axis=0, tiled=True).astype(jnp.float32)
    )
    grad_total = lax.psum(grad_local, "dom")
    return (hidden, grad_total[:cols_dev], grad_total[cols_dev:])


def solution(mesh):
    return jax.shard_map(
        body,
        mesh=mesh,
        in_specs=(
            P("feat", "dom"),
            P("dom"),
            P(None, "dom"),
            P("dom", None),
            P("dom"),
            P("dom"),
            P("feat", None),
            P("feat", None),
            P(),
            P(("dom", "feat"), None),
        ),
        out_specs=(P(("dom", "feat"), None), P("feat", None), P("feat", None)),
        check_vma=False,
    )
```

profile of v0, /device:TPU:32, one launch (start us, length us, event | category | flops | bytes accessed | tf_op | source)
XLA Modules:
  0.0 396.3 jit_solution(11303320467679522365)
XLA Ops:
  7.2 0.7 fusion.5
  8.0 0.8 select_reduce_fusion
  9.5 5.7 %scatter_fusion = s32[16,8]{0,1:T(8,128)S(1)} fusion(s32[16,8]{0,1:T(8,128)S(1)} %broadcast_in_dim.18, s32[64]{0:T(128)S(1)} %get-tuple-element.8, s32[64]{0:T(128)} %param.14), kind=kCustom, calls=%fused_computation.4 | custom fusion | bytes 1280 | tf_op jit(solution)/shard_map/scatter | solution.py:57
  15.9 7.0 %all-to-all-start = ((s32[16,1,8]{2,1,0:T(1,128)}), s32[16,1,8]{2,1,0:T(1,128)S(1)}, u32[]{:S(2)}, u32[]{:S(2)}) async-start(s32[16,1,8]{2,1,0:T(1,128)} %copy.24), calls=%async_computation | async-start | bytes 16384 | tf_op jit(solution)/shard_map/all_to_all | solution.py:58
  23.0 0.7 fusion.6
  23.7 3.8 copy.23
  27.5 2.9 all-to-all-done
  31.7 6.5 %gather_fusion.1 = f32[128,128,64]{2,1,0:T(8,128)} fusion(f32[64,128,64]{2,1,0:T(8,128)} %bitcast.37, s32[1024]{0:T(1024)S(1)} %pad_clamp_fusion.1), kind=kCustom, calls=%fused_computation.1 | custom fusion | bytes 8389120 | tf_op jit(solution)/shard_map/gather | solution.py:61
  38.2 6.8 %copy.25 = f32[128,128,64]{1,2,0:T(8,128)} copy(f32[128,128,64]{2,1,0:T(8,128)} %gather_fusion.1) | data formatting | bytes 8388608 | tf_op jit(solution)/shard_map/gather | solution.py:61
  45.1 4.7 %all-to-all-start.1 = ((f32[16,8,128,64]{2,3,1,0:T(8,128)}), f32[16,8,128,64]{2,3,1,0:T(8,128)}, u32[]{:S(2)}, u32[]{:S(2)}) async-start(f32[16,8,128,64]{2,3,1,0:T(8,128)} %bitcast.40), calls=%async_computation.1 | async-start | bytes 8388608 | tf_op jit(solution)/shard_map/all_to_all | solution.py:62
  49.9 5.0 %gather_fusion = f32[1024,64]{1,0:T(8,128)S(1)} fusion(f32[8192,64]{1,0:T(8,128)} %bitcast.38, s32[1024]{0:T(1024)S(1)} %fusion.7), kind=kCustom, calls=%fused_computation | custom fusion | bytes 528384 | tf_op jit(solution)/shard_map/gather | solution.py:69
  55.0 55.8 %all-to-all-done.1 = f32[16,8,128,64]{2,3,1,0:T(8,128)} async-done(((f32[16,8,128,64]{2,3,1,0:T(8,128)}), f32[16,8,128,64]{2,3,1,0:T(8,128)}, u32[]{:S(2)}, u32[]{:S(2)}) %all-to-all-start.1) | async-done | bytes 4194336 | tf_op jit(solution)/shard_map/all_to_all | solution.py:62
  110.8 2.9 gather_fusion.2
  113.7 2.7 copy.28
  116.4 7.4 %bitcast_select_fusion = f32[8192,64]{1,0:T(8,128)} fusion(f32[64,128,64]{2,1,0:T(8,128)} %copy.28, pred[8192]{0:T(1024)(128)(4,1)S(1)} %fusion.6), kind=kLoop, calls=%fused_computation.5 | loop fusion | flops 524288 | bytes 4202496 | tf_op jit(solution)/shard_map/jit(_where)/select_n | solution.py:66
  123.8 53.7 %gather_fusion.3 = f32[15360,64]{1,0:T(8,128)} fusion(f32[8192,64]{1,0:T(8,128)} %bitcast_select_fusion, s32[15360]{0:T(1024)S(1)} %broadcast_clamp_fusion), kind=kCustom, calls=%fused_computation.3 | custom fusion | bytes 7925760 | tf_op jit(solution)/shard_map/gather | solution.py:67
  177.5 3.9 reduce_sum.19
  181.5 5.1 %fusion = f32[1024,1024]{1,0:T(8,128)} fusion(f32[64,1024]{1,0:T(8,128)S(1)} %copy-done, f32[64,1024]{1,0:T(8,128)S(1)} %copy-done.1, f32[1024,64]{1,0:T(8,128)S(1)} %broadcast_multiply_fusion, f32[1024,64]{1,0:T(8,128)S(1)} %gather_fusion), kind=kOutput, calls=%fused_computation.7 | convolution fusion | flops 1610874880 | bytes 5242880 | tf_op jit(solution)/shard_map/dot_general | solution.py:27
  186.6 59.8 %reduce-scatter.2.cloned.1.call-done = f32[64,1024]{1,0:T(8,128)} async-done(((f32[1024,1024]{1,0:T(8,128)}), f32[64,1024]{1,0:T(8,128)}) %reduce-scatter.2.cloned.1.call-update) | async-done | bytes 262160 | tf_op jit(solution)/shard_map/reduce_scatter | solution.py:73
  246.4 1.8 multiply_convert_fusion
  248.3 41.5 %all-gather.2.cloned.1.call-done = bf16[1024,1024]{1,0:T(8,128)(2,1)} async-done(((bf16[64,1024]{1,0:T(8,128)(2,1)}), bf16[1024,1024]{1,0:T(8,128)(2,1)}) %all-gather.2.cloned.1.call-update) | async-done | bytes 2097168 | tf_op jit(solution)/shard_map/all_gather | solution.py:79
  289.8 3.7 fusion.4
  293.4 94.4 %all-reduce.2.cloned.1.call-done = f32[128,1024]{1,0:T(8,128)} async-done(((f32[128,1024]{1,0:T(8,128)}), f32[128,1024]{1,0:T(8,128)}) %all-reduce.2.cloned.1.call-update) | async-done | bytes 524304 | tf_op jit(solution)/shard_map/psum | solution.py:81
  387.9 1.9 fusion.14
  (33 shorter events, 3.1 us)
Async XLA Ops:
  15.9 14.5 %all-to-all-start = ((s32[16,1,8]{2,1,0:T(1,128)}), s32[16,1,8]{2,1,0:T(1,128)S(1)}, u32[]{:S(2)}, u32[]{:S(2)}) async-start(s32[16,1,8]{2,1,0:T(1,128)} %copy.24), calls=%async_computation | async-start | bytes 16384 | tf_op jit(solution)/shard_map/all_to_all | solution.py:58
  45.0 4.7 %copy-start.5 = (s32[1024]{0:T(1024)S(1)}, s32[1024]{0:T(1024)}, u32[]{:S(2)}) copy-start(s32[1024]{0:T(1024)} %param.11) | copy-start | bytes 12292
  45.0 4.7 %copy-start.3 = (s32[15,1024]{1,0:T(8,128)S(1)}, s32[15,1024]{1,0:T(8,128)}, u32[]{:S(2)}) copy-start(s32[15,1024]{1,0:T(8,128)} %param.12) | copy-start | bytes 184324
  45.1 65.7 %all-to-all-start.1 = ((f32[16,8,128,64]{2,3,1,0:T(8,128)}), f32[16,8,128,64]{2,3,1,0:T(8,128)}, u32[]{:S(2)}, u32[]{:S(2)}) async-start(f32[16,8,128,64]{2,3,1,0:T(8,128)} %bitcast.40), calls=%async_computation.1 | async-start | bytes 8388608 | tf_op jit(solution)/shard_map/all_to_all | solution.py:62
  49.7 196.7 %reduce-scatter.2.cloned.1.call-start = ((), (), s32[]{:S(2)}) async-start(), calls=%async_computation.3 | async-start | bytes 4456448 | tf_op jit(solution)/shard_map/reduce_scatter | solution.py:73
  177.5 4.0 copy-start
  177.5 4.0 %copy-start.1 = (f32[64,1024]{1,0:T(8,128)S(1)}, f32[64,1024]{1,0:T(8,128)}, u32[]{:S(2)}) copy-start(f32[64,1024]{1,0:T(8,128)} %param.16) | copy-start | bytes 786436
  181.4 65.0 %copy-start.2 = (bf16[64,1024]{1,0:T(8,128)(2,1)S(1)}, bf16[64,1024]{1,0:T(8,128)(2,1)}, u32[]{:S(2)}) copy-start(bf16[64,1024]{1,0:T(8,128)(2,1)} %param.19) | copy-start | bytes 393220
  181.4 65.0 %copy-start.4 = (f32[1024]{0:T(1024)S(1)}, f32[1024]{0:T(1024)}, u32[]{:S(2)}) copy-start(f32[1024]{0:T(1024)} %param.18) | copy-start | bytes 12292
  186.5 103.2 %all-gather.2.cloned.1.call-start = ((), (), s32[]{:S(2)}) async-start(), calls=%async_computation.4 | async-start | bytes 2228224 | tf_op jit(solution)/shard_map/all_gather | solution.py:79
  248.2 139.7 %all-reduce.2.cloned.1.call-start = ((), (), s32[]{:S(2)}) async-start(), calls=%async_computation.5 | async-start | bytes 1048576 | tf_op jit(solution)/shard_map/psum | solution.py:81
Sparse Core Ops, SparseCore 0:
  186.6 59.7 reduce-scatter.1
  248.8 40.9 all-gather.1
  293.6 94.2 all-reduce.1
where the time goes:
time: 397 us; the launch traced here: 396 us
  waiting for transfers between devices  255 us (64%)
  local copies, waits for them, and re-layouts  90.3 us (23%)
  other arithmetic  17 us (4%)
  between operations  13.9 us (4%)
  starting transfers between devices  11.8 us (3%)
  matrix products  8.71 us (2%)
    psum x1, waiting for transfers between devices, body(): grad_total = lax.psum(grad_local, 'dom')  94.4 us
    reduce_scatter x1, waiting for transfers between devices, body(): lax.psum_scatter(product(stacked, weight_cat), 'feat', scatter_dimension=...  59.8 us
    all_to_all x1, waiting for transfers between devices, body(): lax.all_to_all(outgoing, 'dom', split_axis=0, concat_axis=0, tiled=True)  55.8 us
    gather x1, local copies, waits for them, and re-layouts, body(): frontier[neighbours.reshape(-1)].reshape(fanout, seeds_dev, cols_dev)  53.7 us
    all_gather x1, waiting for transfers between devices, body(): lax.all_gather(slope, 'feat', axis=0, tiled=True).astype(jnp.float32)  41.5 us
    gather x2, local copies, waits for them, and re-layouts, body(): block_rows[requested.reshape(-1)].reshape(n_dom, SLOTS, BLOCK, cols_dev)  13.3 us
  transfers between devices with their start and end apart: 5, of which 5 were waited for; matrix products, arithmetic and copies ran while one was open for 2% of the time, Pallas kernels for 0%

commit v1 on v0

--- a/solution.py
+++ b/solution.py
@@ -45,6 +45,12 @@
     out_bias,
     cotangent,
 ):
+
+    def lead_files_for(xs):
+        return jnp.concatenate(
+            lax.all_to_all(jnp.stack(lax.axis_size("feat") * [xs], 0), "feat", 0, 0), 0
+        )
+
     cols_dev = feature_table.shape[0]
     node_rows = feature_table.shape[1]
     n_dom = lax.axis_size("dom")
@@ -75,9 +81,7 @@
     )
     hidden = jax.nn.silu(preact).astype(jnp.bfloat16)
     slope = (cotangent.astype(jnp.float32) * silu_slope(preact)).astype(jnp.bfloat16)
-    grad_local = contract(
-        stacked, lax.all_gather(slope, "feat", axis=0, tiled=True).astype(jnp.float32)
-    )
+    grad_local = contract(stacked, lead_files_for(slope).astype(jnp.float32))
     grad_total = lax.psum(grad_local, "dom")
     return (hidden, grad_total[:cols_dev], grad_total[cols_dev:])
 

time: 397 us -> 411 us (1.035)
  blocking collectives: 0 us -> 55.8 us
  waiting for transfers between devices: 255 us -> 214 us
    all_to_all x0 -> x1, blocking collectives: none -> 55.8 us  [lead_files_for(): lax.all_to_all(jnp.stack(lax.axis_size('feat') * [xs], 0), 'feat', 0, 0)]
    all_gather x1 -> x0, waiting for transfers between devices: 41.5 us -> none  [body(): lax.all_gather(slope, 'feat', axis=0, tiled=True).astype(jnp.float32)]
  transfers between devices with their start and end apart: 5 -> 4, of which waited for: 5 -> 4; matrix products, arithmetic and copies ran while one was open for 2% -> 2% of each run, Pallas kernels for 0% -> 0%
where the time goes in v1:
time: 411 us; the launch traced here: 410 us
  waiting for transfers between devices  214 us (52%)
  local copies, waits for them, and re-layouts  90.2 us (22%)
  blocking collectives  55.8 us (14%)
  other arithmetic  16.9 us (4%)
  between operations  14.2 us (3%)
  starting transfers between devices  11.8 us (3%)
  matrix products  7.16 us (2%)
    psum x1, waiting for transfers between devices, body(): grad_total = lax.psum(grad_local, 'dom')  95 us
    reduce_scatter x1, waiting for transfers between devices, body(): lax.psum_scatter(product(stacked, weight_cat), 'feat', scatter_dimension=...  60 us
    all_to_all x1, waiting for transfers between devices, body(): lax.all_to_all(outgoing, 'dom', split_axis=0, concat_axis=0, tiled=True)  55.8 us
    all_to_all x1, blocking collectives, lead_files_for(): lax.all_to_all(jnp.stack(lax.axis_size('feat') * [xs], 0), 'feat', 0, 0)  55.8 us
    gather x1, local copies, waits for them, and re-layouts, body(): frontier[neighbours.reshape(-1)].reshape(fanout, seeds_dev, cols_dev)  53.3 us
    gather x2, local copies, waits for them, and re-layouts, body(): block_rows[requested.reshape(-1)].reshape(n_dom, SLOTS, BLOCK, cols_dev)  13.3 us
  transfers between devices with their start and end apart: 4, of which 4 were waited for; matrix products, arithmetic and copies ran while one was open for 2% of the time, Pallas kernels for 0%

profile of v1, /device:TPU:32, one launch (start us, length us, event | category | flops | bytes accessed | tf_op | source)
XLA Modules:
  0.0 409.8 jit_solution(4215387338329041037)
XLA Ops:
  7.2 0.7 fusion.5
  8.0 0.8 select_reduce_fusion
  9.5 5.7 %scatter_fusion = s32[16,8]{0,1:T(8,128)S(1)} fusion(s32[16,8]{0,1:T(8,128)S(1)} %broadcast_in_dim.18, s32[64]{0:T(128)S(1)} %get-tuple-element.8, s32[64]{0:T(128)} %param.14), kind=kCustom, calls=%fused_computation.4 | custom fusion | bytes 1280 | tf_op jit(solution)/shard_map/scatter | solution.py:63
  15.9 7.0 %all-to-all-start = ((s32[16,1,8]{2,1,0:T(1,128)}), s32[16,1,8]{2,1,0:T(1,128)S(1)}, u32[]{:S(2)}, u32[]{:S(2)}) async-start(s32[16,1,8]{2,1,0:T(1,128)} %copy.24), calls=%async_computation | async-start | bytes 16384 | tf_op jit(solution)/shard_map/all_to_all | solution.py:64
  23.0 0.7 fusion.6
  23.7 3.8 copy.23
  27.5 2.9 all-to-all-done
  31.7 6.5 %gather_fusion.1 = f32[128,128,64]{2,1,0:T(8,128)} fusion(f32[64,128,64]{2,1,0:T(8,128)} %bitcast.38, s32[1024]{0:T(1024)S(1)} %pad_clamp_fusion.1), kind=kCustom, calls=%fused_computation.1 | custom fusion | bytes 8389120 | tf_op jit(solution)/shard_map/gather | solution.py:67
  38.2 6.8 %copy.25 = f32[128,128,64]{1,2,0:T(8,128)} copy(f32[128,128,64]{2,1,0:T(8,128)} %gather_fusion.1) | data formatting | bytes 8388608 | tf_op jit(solution)/shard_map/gather | solution.py:67
  45.1 4.7 %all-to-all-start.1 = ((f32[16,8,128,64]{2,3,1,0:T(8,128)}), f32[16,8,128,64]{2,3,1,0:T(8,128)}, u32[]{:S(2)}, u32[]{:S(2)}) async-start(f32[16,8,128,64]{2,3,1,0:T(8,128)} %bitcast.41), calls=%async_computation.1 | async-start | bytes 8388608 | tf_op jit(solution)/shard_map/all_to_all | solution.py:68
  49.9 5.0 %gather_fusion = f32[1024,64]{1,0:T(8,128)S(1)} fusion(f32[8192,64]{1,0:T(8,128)} %bitcast.39, s32[1024]{0:T(1024)S(1)} %fusion.7), kind=kCustom, calls=%fused_computation | custom fusion | bytes 528384 | tf_op jit(solution)/shard_map/gather | solution.py:75
  55.0 55.8 %all-to-all-done.1 = f32[16,8,128,64]{2,3,1,0:T(8,128)} async-done(((f32[16,8,128,64]{2,3,1,0:T(8,128)}), f32[16,8,128,64]{2,3,1,0:T(8,128)}, u32[]{:S(2)}, u32[]{:S(2)}) %all-to-all-start.1) | async-done | bytes 4194336 | tf_op jit(solution)/shard_map/all_to_all | solution.py:68
  110.8 2.9 gather_fusion.2
  113.7 2.7 copy.28
  116.4 7.4 %bitcast_select_fusion = f32[8192,64]{1,0:T(8,128)} fusion(f32[64,128,64]{2,1,0:T(8,128)} %copy.28, pred[8192]{0:T(1024)(128)(4,1)S(1)} %fusion.6), kind=kLoop, calls=%fused_computation.5 | loop fusion | flops 524288 | bytes 4202496 | tf_op jit(solution)/shard_map/jit(_where)/select_n | solution.py:72
  123.8 53.3 %gather_fusion.3 = f32[15360,64]{1,0:T(8,128)} fusion(f32[8192,64]{1,0:T(8,128)} %bitcast_select_fusion, s32[15360]{0:T(1024)S(1)} %broadcast_clamp_fusion), kind=kCustom, calls=%fused_computation.3 | custom fusion | bytes 7925760 | tf_op jit(solution)/shard_map/gather | solution.py:73
  177.1 3.9 reduce_sum.19
  181.1 5.1 %fusion = f32[1024,1024]{1,0:T(8,128)} fusion(f32[64,1024]{1,0:T(8,128)S(1)} %copy-done, f32[64,1024]{1,0:T(8,128)S(1)} %copy-done.1, f32[1024,64]{1,0:T(8,128)S(1)} %broadcast_multiply_fusion, f32[1024,64]{1,0:T(8,128)S(1)} %gather_fusion), kind=kOutput, calls=%fused_computation.7 | convolution fusion | flops 1610874880 | bytes 5242880 | tf_op jit(solution)/shard_map/dot_general | solution.py:27
  186.2 60.0 %reduce-scatter.2.cloned.1.call-done = f32[64,1024]{1,0:T(8,128)} async-done(((f32[1024,1024]{1,0:T(8,128)}), f32[64,1024]{1,0:T(8,128)}) %reduce-scatter.2.cloned.1.call-update) | async-done | bytes 262160 | tf_op jit(solution)/shard_map/reduce_scatter | solution.py:79
  246.3 1.7 multiply_convert_fusion
  248.2 55.8 %all_to_all.19 = bf16[16,64,1024]{2,1,0:T(8,128)(2,1)S(1)} all-to-all(bf16[16,64,1024]{2,1,0:T(8,128)(2,1)S(1)} %stack.2), channel_id=1, replica_groups=mesh['dom'=16,'feat'=16] {'feat'}, dimensions={0} | all-to-all | bytes 4194304 | tf_op jit(solution)/shard_map/all_to_all | solution.py:51
  304.0 2.1 fusion.4
  306.1 95.0 %all-reduce.2.cloned.1.call-done = f32[128,1024]{1,0:T(8,128)} async-done(((f32[128,1024]{1,0:T(8,128)}), f32[128,1024]{1,0:T(8,128)}) %all-reduce.2.cloned.1.call-update) | async-done | bytes 524304 | tf_op jit(solution)/shard_map/psum | solution.py:85
  401.1 1.9 fusion.14
  (32 shorter events, 3.3 us)
Async XLA Ops:
  15.9 14.5 %all-to-all-start = ((s32[16,1,8]{2,1,0:T(1,128)}), s32[16,1,8]{2,1,0:T(1,128)S(1)}, u32[]{:S(2)}, u32[]{:S(2)}) async-start(s32[16,1,8]{2,1,0:T(1,128)} %copy.24), calls=%async_computation | async-start | bytes 16384 | tf_op jit(solution)/shard_map/all_to_all | solution.py:64
  45.1 4.7 %copy-start.5 = (s32[1024]{0:T(1024)S(1)}, s32[1024]{0:T(1024)}, u32[]{:S(2)}) copy-start(s32[1024]{0:T(1024)} %param.11) | copy-start | bytes 12292
  45.1 4.8 %copy-start.3 = (s32[15,1024]{1,0:T(8,128)S(1)}, s32[15,1024]{1,0:T(8,128)}, u32[]{:S(2)}) copy-start(s32[15,1024]{1,0:T(8,128)} %param.12) | copy-start | bytes 184324
  45.1 65.8 %all-to-all-start.1 = ((f32[16,8,128,64]{2,3,1,0:T(8,128)}), f32[16,8,128,64]{2,3,1,0:T(8,128)}, u32[]{:S(2)}, u32[]{:S(2)}) async-start(f32[16,8,128,64]{2,3,1,0:T(8,128)} %bitcast.41), calls=%async_computation.1 | async-start | bytes 8388608 | tf_op jit(solution)/shard_map/all_to_all | solution.py:68
  49.7 196.5 %reduce-scatter.2.cloned.1.call-start = ((), (), s32[]{:S(2)}) async-start(), calls=%async_computation.4 | async-start | bytes 4456448 | tf_op jit(solution)/shard_map/reduce_scatter | solution.py:79
  177.1 4.0 copy-start
  177.1 4.0 copy-start.1
  181.1 65.2 %copy-start.2 = (bf16[64,1024]{1,0:T(8,128)(2,1)S(1)}, bf16[64,1024]{1,0:T(8,128)(2,1)}, u32[]{:S(2)}) copy-start(bf16[64,1024]{1,0:T(8,128)(2,1)} %param.19) | copy-start | bytes 393220
  181.1 65.2 %copy-start.4 = (f32[1024]{0:T(1024)S(1)}, f32[1024]{0:T(1024)}, u32[]{:S(2)}) copy-start(f32[1024]{0:T(1024)} %param.18) | copy-start | bytes 12292
  186.2 214.9 %all-reduce.2.cloned.1.call-start = ((), (), s32[]{:S(2)}) async-start(), calls=%async_computation.5 | async-start | bytes 1048576 | tf_op jit(solution)/shard_map/psum | solution.py:85
Sparse Core Ops, SparseCore 0:
  186.3 59.9 reduce-scatter.1
  306.3 94.8 all-reduce.1
